TPU v7x, 512 devices: a whole 4x4x16 slice. The times are simulated.
512 devices in a mesh: replica: 32 (over z, x_lo), fsdp: 16 (over x_hi, y, core).
Axes of the slice: x: 4 (x_hi: 2, x_lo: 2; x = x_hi * 2 + x_lo), y: 4, z: 16, core: 2. Of those that a mesh axis runs over, the one named last changes fastest.
Arguments:
- tokens: bfloat16 [32, 2048, 8192], P('replica', 'fsdp'), may hold values from -6 to 6
- norm_gain: float32 [8192], replicated, may hold values from 0.1 to 1.9
- weight: bfloat16 [32, 8192, 768], P('replica', 'fsdp'), may hold values from -0.0625 to 0.0625
- momentum: float32 [32, 8192, 128], P('replica', 'fsdp'), may hold values from -0.03 to 0.03
- cotangent: bfloat16 [32, 2048, 768], P('replica', 'fsdp'), may hold values from -6 to 6
- fragment: int32 [32], replicated, may hold values from 0 to 5
- partner: int32 [32], replicated, may hold values from 0 to 31, as said below
Outputs:
- keys: bfloat16 [32, 2048, 768], P('replica', 'fsdp')
- new_weight: bfloat16 [32, 8192, 768], P('replica', 'fsdp')
- new_momentum: float32 [32, 8192, 128], P('replica', 'fsdp')
Inputs may be any that keep to these rules, and one draw needn't show every extreme that they name: partner is a perfect matching: partner[partner[r]] == r and partner[r] != r.
All inputs are finite; a program needn't handle non-finite values.
Results may differ from a plain program's by a relative error of at most 0.0049.
Values may be sent and summed in bfloat16 or wider, within the bound.
A program may use at most 128 MiB of HBM per device.

v0:
```python
import jax
import jax.numpy as jnp
from jax import lax
from jax.sharding import PartitionSpec as P

HD = 128


inner_rate = 0.0001
outer_rate = 0.7
beta_value = 0.9


def body(tokens, norm_gain, weight, momentum, cotangent, fragment, partner):
    values = tokens[0].astype(jnp.float32)
    scale = lax.rsqrt(jnp.mean(values * values, axis=-1, keepdims=True) + 1e-05)
    normed = (values * scale * norm_gain).astype(jnp.bfloat16)
    local_weight = weight[0]
    spread = lax.all_to_all(normed, "fsdp", split_axis=1, concat_axis=0, tiled=True)
    block = normed
    key_sum = jnp.dot(
        block,
        lax.all_gather(local_weight, "fsdp", axis=0, tiled=True),
        preferred_element_type=jnp.float32,
    )
    keys = key_sum.astype(jnp.bfloat16)
    block = spread
    grad = lax.dot_general(
        block,
        lax.all_gather(cotangent[0], "fsdp", axis=0, tiled=True),
        (((0,), (0,)), ((), ())),
        preferred_element_type=jnp.float32,
    )
    myself = lax.axis_index("replica")
    mate = partner[myself]
    offset = fragment[jnp.minimum(myself, mate)] * HD
    delta = (inner_rate * lax.dynamic_slice_in_dim(grad, offset, HD, 1)).astype(jnp.bfloat16)
    piece = lax.all_gather(delta[None], "replica", axis=0, tiled=True)
    owners = jnp.arange(piece.shape[0], dtype=jnp.int32)
    chosen = (owners == mate)[:, None, None]
    other = jnp.sum(jnp.where(chosen, piece.astype(jnp.float32), 0.0), axis=0)
    mix = (delta.astype(jnp.float32) + other) * 0.5
    new_momentum = beta_value * momentum[0] + mix
    anchor = local_weight.astype(jnp.float32)
    inner = anchor - inner_rate * grad
    frag_anchor = lax.dynamic_slice_in_dim(anchor, offset, HD, 1)
    outer = frag_anchor - outer_rate * (beta_value * new_momentum + mix)
    new_weight = lax.dynamic_update_slice_in_dim(inner, outer, offset, 1).astype(jnp.bfloat16)
    return (keys[None], new_weight[None], new_momentum[None])


def solution(mesh):
    in_specs = (
        P("replica", "fsdp", None),
        P(),
        P("replica", "fsdp", None),
        P("replica", "fsdp", None),
        P("replica", "fsdp", None),
        P(),
        P(),
    )
    out_specs = (P("replica", "fsdp", None), P("replica", "fsdp", None), P("replica", "fsdp", None))
    return jax.shard_map(body, mesh=mesh, in_specs=in_specs, out_specs=out_specs, check_vma=False)
```

profile of v0, /device:TPU:1, one launch (start us, length us, event | category | flops | bytes accessed | tf_op | source)
XLA Modules:
  0.0 363.2 jit_solution(9357123821922233631)
XLA Ops:
  7.2 0.0 all-gather.9.cloned.1.call-start
  7.2 0.7 all-gather.9.cloned.1.call-update
  7.9 0.0 copy-start.1
  7.9 3.2 copy.10
  11.1 0.0 copy-done.1
  11.2 1.1 fusion.3
  12.3 2.2 multiply_convert_fusion
  14.5 0.0 copy-start.4
  14.5 0.0 copy-start.5
  14.5 11.2 %all-to-all-start = ((bf16[128,16,512]{0,2,1:T(8,128)(2,1)}), bf16[128,16,512]{0,2,1:T(8,128)(2,1)}, u32[]{:S(2)}, u32[]{:S(2)}) async-start(bf16[128,16,512]{0,2,1:T(8,128)(2,1)} %multiply_convert_fusion), calls=%async_computation | async-start | bytes 4194304 | tf_op jit(solution)/shard_map/all_to_all | solution.py:19
  25.7 0.0 all-gather.11.cloned.1.call-start
  25.7 0.0 copy-done.4
  25.7 0.6 dynamic_slice.12
  27.0 0.0 copy-done.5
  27.0 0.6 dynamic_slice.13
  28.2 28.2 %all-to-all-done = bf16[128,16,512]{0,2,1:T(8,128)(2,1)} async-done(((bf16[128,16,512]{0,2,1:T(8,128)(2,1)}), bf16[128,16,512]{0,2,1:T(8,128)(2,1)}, u32[]{:S(2)}, u32[]{:S(2)}) %all-to-all-start) | async-done | bytes 2097184 | tf_op jit(solution)/shard_map/all_to_all | solution.py:19
  56.5 0.0 copy-start
  56.5 4.0 %copy.11 = bf16[16,128,512]{2,1,0:T(8,128)(2,1)} copy(bf16[16,128,512]{1,2,0:T(8,128)(2,1)} %bitcast.5) | data formatting | bytes 4194304 | tf_op jit(solution)/shard_map/all_to_all | solution.py:19
  60.4 35.0 %all-gather.9.cloned.1.call-done = bf16[1,2048,768]{2,1,0:T(8,128)(2,1)} async-done(((bf16[1,128,768]{2,1,0:T(8,128)(2,1)}), bf16[1,2048,768]{2,1,0:T(8,128)(2,1)}) %all-gather.9.cloned.1.call-update) | async-done | bytes 3145744 | tf_op jit(solution)/shard_map/all_gather | solution.py:30
  95.4 0.0 copy-done
  95.4 5.3 %bitcast_subtract_fusion = (bf16[512,768]{1,0:T(8,128)(2,1)}, f32[512,768]{1,0:T(8,128)S(1)}) fusion(bf16[1,512,768]{2,1,0:T(8,128)(2,1)S(1)} %copy-done, bf16[2048,512]{1,0:T(8,128)(2,1)} %bitcast.56, bf16[1,2048,768]{2,1,0:T(8,128)(2,1)} %all-gather.9.cloned.1.call-done), kind=kOutput, calls=%fused_computation.15 | convolution fusion | flops 1612185600 | bytes 8388608 | tf_op jit(solution)/shard_map/dot_general | solution.py:28
  100.7 0.0 copy-start.3
  100.7 1.2 copy-done.3
  101.9 0.7 multiply_convert_fusion.1
  102.5 0.0 all-gather.11.cloned.1.call-update
  102.6 0.0 all-gather.7.cloned.1.call-start
  102.6 0.7 all-gather.7.cloned.1.call-update
  103.3 2.4 convert_element_type.50
  105.7 0.6 iota_compare_fusion
  106.4 116.8 %all-gather.11.cloned.1.call-done = bf16[16384,128]{1,0:T(8,128)(2,1)} async-done(((bf16[512,128]{1,0:T(8,128)(2,1)}), bf16[16384,128]{1,0:T(8,128)(2,1)}) %all-gather.11.cloned.1.call-update) | async-done | bytes 4194320 | tf_op jit(solution)/shard_map/all_gather | solution.py:38
  223.2 0.0 copy-start.2
  223.2 3.3 fusion.2
  226.5 0.0 copy-done.2
  226.5 1.9 fusion.23
  228.4 119.9 %all-gather.7.cloned.1.call-done = bf16[1,8192,768]{2,1,0:T(8,128)(2,1)} async-done(((bf16[1,512,768]{2,1,0:T(8,128)(2,1)}), bf16[1,8192,768]{2,1,0:T(8,128)(2,1)}) %all-gather.7.cloned.1.call-update) | async-done | bytes 12582928 | tf_op jit(solution)/shard_map/all_gather | solution.py:23
  348.3 8.4 %fusion.17 = bf16[1,128,768]{2,1,0:T(8,128)(2,1)} fusion(bf16[1,8192,768]{2,1,0:T(8,128)(2,1)} %all-gather.7.cloned.1.call-done, bf16[1,128,8192]{1,2,0:T(8,128)(2,1)S(1)} %copy.10, f32[8192]{0:T(1024)S(1)} %copy-done.1, f32[128]{0:T(128)S(1)} %add_rsqrt_fusion), kind=kOutput, calls=%fused_computation.17 | convolution fusion | flops 1614905344 | bytes 14909952 | tf_op jit(solution)/shard_map/dot_general | solution.py:21
  (2 shorter events, 0.0 us)
Async XLA Ops:
  7.2 88.2 %all-gather.9.cloned.1.call-start = ((), (), s32[]{:S(2)}) async-start(), calls=%async_computation.2 | async-start | bytes 3342336 | tf_op jit(solution)/shard_map/all_gather | solution.py:30
  7.9 3.2 copy-start.1
  14.5 11.2 %copy-start.4 = (s32[32]{0:T(128)S(1)}, s32[32]{0:T(128)}, u32[]{:S(2)}) copy-start(s32[32]{0:T(128)} %param.13) | copy-start | bytes 388
  14.5 12.5 %copy-start.5 = (s32[32]{0:T(128)S(1)}, s32[32]{0:T(128)}, u32[]{:S(2)}) copy-start(s32[32]{0:T(128)} %param.12) | copy-start | bytes 388
  14.5 41.9 %all-to-all-start = ((bf16[128,16,512]{0,2,1:T(8,128)(2,1)}), bf16[128,16,512]{0,2,1:T(8,128)(2,1)}, u32[]{:S(2)}, u32[]{:S(2)}) async-start(bf16[128,16,512]{0,2,1:T(8,128)(2,1)} %multiply_convert_fusion), calls=%async_computation | async-start | bytes 4194304 | tf_op jit(solution)/shard_map/all_to_all | solution.py:19
  25.7 197.5 %all-gather.11.cloned.1.call-start = ((), (), s32[]{:S(2)}) async-start(), calls=%async_computation.3 | async-start | bytes 4325376 | tf_op jit(solution)/shard_map/all_gather | solution.py:38
  56.5 39.0 %copy-start = (bf16[1,512,768]{2,1,0:T(8,128)(2,1)S(1)}, bf16[1,512,768]{2,1,0:T(8,128)(2,1)}, u32[]{:S(2)}) copy-start(bf16[1,512,768]{2,1,0:T(8,128)(2,1)} %param.9) | copy-start | bytes 2359300
  100.7 1.2 copy-start.3
  102.6 245.7 %all-gather.7.cloned.1.call-start = ((), (), s32[]{:S(2)}) async-start(), calls=%async_computation.1 | async-start | bytes 13369344 | tf_op jit(solution)/shard_map/all_gather | solution.py:23
  223.2 3.3 copy-start.2
Sparse Core Ops, SparseCore 0:
  11.4 84.0 all-gather.8
  102.7 120.4 all-gather.10
  226.5 121.7 all-gather.6
where the time goes:
time: 364 us; the launch traced here: 363 us
  waiting for transfers between devices  301 us (83%)
  between operations  15.1 us (4%)
  matrix products  13.7 us (4%)
  other arithmetic  12.2 us (3%)
  starting transfers between devices  11.3 us (3%)
  local copies, waits for them, and re-layouts  9.56 us (3%)
    all_gather x1, waiting for transfers between devices, body(): lax.all_gather(local_weight, 'fsdp', axis=0, tiled=True)  120 us
    all_gather x1, waiting for transfers between devices, body(): piece = lax.all_gather(delta[None], 'replica', axis=0, tiled=True)  117 us
    all_gather x1, waiting for transfers between devices, body(): lax.all_gather(cotangent[0], 'fsdp', axis=0, tiled=True)  35 us
    all_to_all x1, waiting for transfers between devices, body(): lax.all_to_all(normed, 'fsdp', split_axis=1, concat_axis=0, tiled=True)  28.2 us
    all_to_all x1, starting transfers between devices, body(): lax.all_to_all(normed, 'fsdp', split_axis=1, concat_axis=0, tiled=True)  11.2 us
    dot_general x1, matrix products, body(): jnp.dot(block, lax.all_gather(local_weight, 'fsdp', axis=0, tiled=True),...  8.41 us
  transfers between devices with their start and end apart: 4, of which 4 were waited for; matrix products, arithmetic and copies ran while one was open for 5% of the time, Pallas kernels for 0%

commit v1 on v0

v1 whole, which is shorter than its diff:
```python
import jax
import jax.numpy as jnp
from jax import lax
from jax.experimental import pallas as pl
from jax.experimental.pallas import tpu as pltpu
from jax.sharding import PartitionSpec as P

HD = 128
NC = 4
MESH = pl.DeviceIdType.MESH
F32 = jnp.float32
BF16 = jnp.bfloat16

inner_rate = 0.0001
outer_rate = 0.7
beta_value = 0.9


def kernel(
    tokens, gain, weight, momentum, cot, fragment, partner_row, partner,
    keys_o, nw_o, nm_o,
    tok, scale, S, R, W2, C, Gt, Gs, Gr, Pacc, Ps, Pr, Ss, Sr, D, X1, X2s, X2r, mom, fragv,
    lsem, a_s, a_r, w_s, w_r, c_s, c_r, f_s, f_r, g_s, g_r, p_s, p_r, k_s, k_r, x1_s, x1_r, x2_s, x2_r,
):
    r = lax.axis_index("replica")
    f = lax.axis_index("fsdp")
    xh = f // 8
    q = f % 8
    y = q // 2
    c = q % 2
    z = r // 2

    def dev(q2):
        return (r, xh * 8 + q2)

    xpart = (r, (1 - xh) * 8 + q)
    sib = dev(y * 2 + 1 - c)

    tok_cp = [
        pltpu.make_async_copy(tokens.at[pl.ds(h * 32, 32)], tok.at[pl.ds(h * 32, 32)], lsem.at[h])
        for h in range(4)
    ]
    c_cp = pltpu.make_async_copy(cot, C.at[q], lsem.at[4])
    w_cp = pltpu.make_async_copy(weight, W2.at[:, xh], lsem.at[5])
    m_cp = pltpu.make_async_copy(momentum, mom, lsem.at[6])
    c_cp.start()
    w_cp.start()
    for cp in tok_cp:
        cp.start()
    m_cp.start()

    bar = pltpu.get_barrier_semaphore()
    for k in range(1, 8):
        pl.semaphore_signal(bar, inc=1, device_id=dev((q + k) % 8), device_id_type=MESH)
    pl.semaphore_signal(bar, inc=1, device_id=xpart, device_id_type=MESH)

    def greet(k, _):
        pl.semaphore_signal(bar, inc=1, device_id=((r + k) % 32, f), device_id_type=MESH)
        return 0

    lax.fori_loop(1, 32, greet, 0)
    pl.semaphore_wait(bar, 39)

    def c_send(k):
        if k == 0:
            to = sib
        else:
            to = dev(((y + k) % 4) * 2 + c)
        return pltpu.make_async_remote_copy(
            src_ref=C.at[q], dst_ref=C.at[q], send_sem=c_s.at[k], recv_sem=c_r.at[k], device_id=to, device_id_type=MESH)

    c_cp.wait()
    for k in (2, 1, 3, 0):
        c_send(k).start()

    def w_send(i):
        return pltpu.make_async_remote_copy(
            src_ref=W2.at[i, xh], dst_ref=W2.at[i, xh], send_sem=w_s.at[i], recv_sem=w_r.at[i], device_id=xpart,
            device_id_type=MESH)

    w_cp.wait()
    for i in range(NC):
        w_send(i).start()

    for cp in tok_cp:
        cp.wait()

    def rows(t, _):
        v = tok[pl.ds(pl.multiple_of(t * 16, 16), 16), :].astype(F32)
        m = jnp.sum(v * v, axis=-1, keepdims=True) * (1.0 / 8192)
        scale[pl.ds(pl.multiple_of(t * 16, 16), 16), :] = jnp.broadcast_to(lax.rsqrt(m + 1e-05), (16, 128))
        return 0

    lax.fori_loop(0, 8, rows, 0)

    def a_send(i, k):
        q2 = (q + k) % 8
        return pltpu.make_async_remote_copy(
            src_ref=S.at[i, q2], dst_ref=R.at[i, q], send_sem=a_s.at[i, k], recv_sem=a_r.at[i, k], device_id=dev(q2),
            device_id_type=MESH)

    def norm_chunk(i):
        def one(b, _):
            for h in range(2):
                col = pl.multiple_of(h * 4096 + b * 512 + i * 128, 128)
                v = tok[:, pl.ds(col, 128)].astype(F32)
                S[i, b, :, h * 128:(h + 1) * 128] = (v * scale[...] * gain[:, pl.ds(col, 128)]).astype(BF16)
            return 0

        lax.fori_loop(0, 8, one, 0)
        R[i, q] = S[i, q]

    def send_chunk(i):
        def one(k, _):
            a_send(i, k).start()
            return 0

        lax.fori_loop(1, 8, one, 0)

    for i in range(NC):
        norm_chunk(i)
        if i < 2:
            send_chunk(i)

    def c_pass(k):
        slot = ((y + 4 - k) % 4) * 2 + c
        return pltpu.make_async_remote_copy(
            src_ref=C.at[slot], dst_ref=C.at[slot], send_sem=f_s.at[k], recv_sem=f_r.at[k], device_id=sib,
            device_id_type=MESH)

    for k in (1, 3, 2):
        c_send(k).wait_recv()
        c_pass(k).start()
    c_send(0).wait_recv()
    for k in (1, 3, 2):
        c_pass(k).wait_recv()

    lane = lax.broadcasted_iota(jnp.int32, (8, 32), 1).astype(F32)
    mine = r.astype(F32)
    partners = jnp.broadcast_to(partner_row[...].astype(F32), (8, 32))
    mate = jnp.sum(jnp.where(lane == mine, partners, 0.0), axis=-1, keepdims=True)
    fragments = jnp.broadcast_to(fragment[...].astype(F32), (8, 32))
    frag_at = jnp.sum(jnp.where(lane == jnp.minimum(mate, mine), fragments, 0.0), axis=-1, keepdims=True)
    fragv[...] = jnp.broadcast_to(frag_at, (8, HD))

    def g_send(i):
        return pltpu.make_async_remote_copy(
            src_ref=Gs.at[i], dst_ref=Gr.at[i], send_sem=g_s.at[i], recv_sem=g_r.at[i], device_id=xpart,
            device_id_type=MESH)

    def x1_send(i, k):
        j = 8 * (k // 2) + 2 * i + k % 2
        return j, pltpu.make_async_remote_copy(
            src_ref=D.at[i, k], dst_ref=X1.at[r], send_sem=x1_s, recv_sem=x1_r, device_id=(j, f), device_id_type=MESH)

    def finalize(i):
        g_send(i).wait_recv()
        Gt[i, xh] = Gt[i, xh] + Gr[i].astype(F32)
        frag = jnp.broadcast_to(fragv[0:1, :], (128, HD))
        cut = Gt[i, xh, :, 0:HD]
        for j in range(1, 6):
            cut = jnp.where(frag == float(j), Gt[i, xh, :, j * HD:(j + 1) * HD], cut)
        d = (inner_rate * cut).astype(BF16)
        D[i] = d.reshape(8, 16, HD)

        def one(k, _):
            j, cp = x1_send(i, k)

            @pl.when(j != r)
            def _():
                cp.start()

            @pl.when(j == r)
            def _():
                X1[r] = D[i, k]

            return 0

        lax.fori_loop(0, 8, one, 0)

    my_piece = 2 * (z // 4) + r % 2
    my_chunk = z % 4

    def x2_send(k):
        d = (r + k) % 32
        return pltpu.make_async_remote_copy(
            src_ref=X2s.at[d], dst_ref=X2r.at[my_chunk, my_piece], send_sem=x2_s, recv_sem=x2_r.at[my_chunk],
            device_id=(d, f), device_id_type=MESH)

    def relay(i):
        @pl.when(my_chunk == i)
        def _():
            whole = X1.at[pl.ds(0, 31)]
            pltpu.make_async_copy(whole, whole, x1_r).wait()

            def pick(d, _):
                X2s[d] = X1[partner[d]]
                return 0

            lax.fori_loop(0, 32, pick, 0)

            def one(k, _):
                x2_send(k).start()
                return 0

            lax.fori_loop(1, 32, one, 0)
            X2r[i, my_piece] = X2s[r]

    def step(t, _):
        def arrive(k, _):
            a_send(t, k).wait_recv()
            return 0

        lax.fori_loop(1, 8, arrive, 0)

        @pl.when(t < NC - 2)
        def _():
            send_chunk(t + 2)

        lhs = R[t].reshape(1024, 256)
        for n in range(3):
            cols = slice(n * 256, (n + 1) * 256)
            g = lax.dot_general(lhs, C[:, :, cols].reshape(1024, 256), (((0,), (0,)), ((), ())), preferred_element_type=F32)
            Gt[t, :, :, cols] = g.reshape(2, 128, 256)
        Gs[t] = Gt[t, 1 - xh].astype(BF16)
        g_send(t).start()

        @pl.when(t >= 1)
        def _():
            finalize(t - 1)

        @pl.when(t >= 2)
        def _():
            relay(t - 2)

        w_send(t).wait_recv()

        @pl.when(t == 0)
        def _():
            Pacc[...] = jnp.zeros_like(Pacc)

        for n in range(3):
            cols = slice(n * 256, (n + 1) * 256)
            p = jnp.dot(lhs, W2[t, :, :, cols].reshape(256, 256), preferred_element_type=F32)
            Pacc[:, :, cols] += p.reshape(8, 128, 256)
        return 0

    lax.fori_loop(0, NC, step, 0)

    p_send = pltpu.make_async_remote_copy(
        src_ref=Ps, dst_ref=Pr, send_sem=p_s, recv_sem=p_r, device_id=sib, device_id_type=MESH)
    for b in range(4):
        Ps[b] = Pacc[b * 2 + 1 - c].astype(BF16)
    p_send.start()
    finalize(NC - 1)
    relay(NC - 2)

    def k_send(k):
        y2 = (y + k) % 4
        return pltpu.make_async_remote_copy(
            src_ref=Ss.at[y2], dst_ref=Sr.at[k - 1], send_sem=k_s.at[k], recv_sem=k_r.at[k], device_id=dev(y2 * 2 + c),
            device_id_type=MESH)

    p_send.wait_recv()
    for k in (2, 1, 3):
        y2 = (y + k) % 4
        Ss[y2] = (Pacc[y2 * 2 + c] + Pr[y2].astype(F32)).astype(BF16)
        k_send(k).start()
    own = Pacc[q] + Pr[y].astype(F32)
    relay(NC - 1)

    m_cp.wait()
    for k in (1, 3, 2):
        k_send(k).wait_recv()
    keys_o[...] = (own + Sr[0].astype(F32) + Sr[1].astype(F32) + Sr[2].astype(F32)).astype(BF16)

    def update(i, _):
        @pl.when(my_chunk == i)
        def _():
            part = X2r.at[i, pl.ds(0, 7)]
            pltpu.make_async_copy(part, part, x2_r.at[i]).wait()

        @pl.when(my_chunk != i)
        def _():
            part = X2r.at[i]
            pltpu.make_async_copy(part, part, x2_r.at[i]).wait()

        here = pl.ds(pl.multiple_of(i * 128, 128), 128)
        delta = D[i].reshape(128, HD).astype(F32)
        mix = (delta + X2r[i].reshape(128, HD).astype(F32)) * 0.5
        nm = beta_value * mom[here, :] + mix
        nm_o[here, :] = nm
        frag = jnp.broadcast_to(fragv[0:1, :], (128, HD))
        step_out = outer_rate * (beta_value * nm + mix)
        for j in range(6):
            cols = slice(j * HD, (j + 1) * HD)
            change = jnp.where(frag == float(j), step_out, inner_rate * Gt[i, xh, :, cols])
            nw_o[here, cols] = (W2[i, xh, :, cols].astype(F32) - change).astype(BF16)
        return 0

    lax.fori_loop(0, NC, update, 0)

    for k in range(4):
        c_send(k).wait_send()
    for k in (1, 2, 3):
        c_pass(k).wait_send()
        k_send(k).wait_send()
    p_send.wait_send()

    def sent(i, _):
        w_send(i).wait_send()
        g_send(i).wait_send()

        def one(k, _):
            a_send(i, k).wait_send()
            return 0

        lax.fori_loop(1, 8, one, 0)
        return 0

    lax.fori_loop(0, NC, sent, 0)
    most = X1.at[pl.ds(0, 31)]
    pltpu.make_async_copy(most, most, x1_s).wait()
    pltpu.make_async_copy(most, most, x2_s).wait()


def body(tokens, norm_gain, weight, momentum, cotangent, fragment, partner):
    any_, vmem, smem = (pl.BlockSpec(memory_space=m) for m in (pl.ANY, pltpu.VMEM, pltpu.SMEM))
    V = pltpu.VMEM
    dma = pltpu.SemaphoreType.DMA
    keys, nw, nm = pl.pallas_call(
        kernel,
        out_shape=(
            jax.ShapeDtypeStruct((128, 768), BF16),
            jax.ShapeDtypeStruct((512, 768), BF16),
            jax.ShapeDtypeStruct((512, HD), F32),
        ),
        in_specs=[any_, vmem, any_, any_, any_, vmem, vmem, smem],
        out_specs=(vmem, vmem, vmem),
        scratch_shapes=[
            V((128, 8192), BF16),
            V((128, 128), F32),
            V((NC, 8, 128, 256), BF16),
            V((NC, 8, 128, 256), BF16),
            V((NC, 2, 128, 768), BF16),
            V((8, 128, 768), BF16),
            V((NC, 2, 128, 768), F32),
            V((NC, 128, 768), BF16),
            V((NC, 128, 768), BF16),
            V((8, 128, 768), F32),
            V((4, 128, 768), BF16),
            V((4, 128, 768), BF16),
            V((4, 128, 768), BF16),
            V((3, 128, 768), BF16),
            V((NC, 8, 16, HD), BF16),
            V((32, 16, HD), BF16),
            V((32, 16, HD), BF16),
            V((NC, 8, 16, HD), BF16),
            V((512, HD), F32),
            V((8, HD), F32),
            dma((7,)),
            dma((NC, 8)), dma((NC, 8)),
            dma((NC,)), dma((NC,)),
            dma((4,)), dma((4,)),
            dma((4,)), dma((4,)),
            dma((NC,)), dma((NC,)),
            dma, dma,
            dma((4,)), dma((4,)),
            dma, dma,
            dma, dma((NC,)),
        ],
        compiler_params=pltpu.CompilerParams(
            collective_id=0, has_side_effects=True, vmem_limit_bytes=48 * 2**20
        ),
    )(tokens[0], norm_gain[None], weight[0].reshape(NC, 128, 768), momentum[0], cotangent[0], fragment[None], partner[None], partner)
    return (keys[None], nw[None], nm[None])


def solution(mesh):
    in_specs = (
        P("replica", "fsdp", None),
        P(),
        P("replica", "fsdp", None),
        P("replica", "fsdp", None),
        P("replica", "fsdp", None),
        P(),
        P(),
    )
    out_specs = (P("replica", "fsdp", None), P("replica", "fsdp", None), P("replica", "fsdp", None))
    return jax.shard_map(body, mesh=mesh, in_specs=in_specs, out_specs=out_specs, check_vma=False)
```

time: 364 us -> 86.2 us (0.24)
  waiting for transfers between devices: 301 us -> 0 us
  Pallas kernels: 0 us -> 75.9 us
  between operations: 15.1 us -> 0.66 us
  matrix products: 13.7 us -> 0 us
  other arithmetic: 12.2 us -> 0 us
  starting transfers between devices: 11.3 us -> 0 us
    all_gather x3 -> x0, waiting for transfers between devices: 272 us -> none  [the longest x1 120 us: body(): lax.all_gather(local_weight, 'fsdp', axis=0, tiled=True)]
    pallas_call x0 -> x1, Pallas kernels: none -> 75.9 us  [body(): pl.pallas_call(kernel, out_shape=(jax.ShapeDtypeStruct((128, 768), BF16),...]
    all_to_all x1 -> x0, waiting for transfers between devices: 28.2 us -> none  [body(): lax.all_to_all(normed, 'fsdp', split_axis=1, concat_axis=0, tiled=True)]
    dot_general x2 -> x0, matrix products: 13.7 us -> none  [the longest x1 8.41 us: body(): jnp.dot(block, lax.all_gather(local_weight, 'fsdp', axis=0, tiled=True),...]
    all_to_all x1 -> x0, starting transfers between devices: 11.2 us -> none  [body(): lax.all_to_all(normed, 'fsdp', split_axis=1, concat_axis=0, tiled=True)]
    convert_element_type x3 -> x0, other arithmetic: 5.3 us -> none  [the longest x1 2.39 us: body(): anchor = local_weight.astype(jnp.float32)]
    unnamed x13 -> x17, local copies, waits for them, and re-layouts: 4.41 us -> 8.92 us
    reduce_sum x2 -> x0, other arithmetic: 4.41 us -> none  [the longest x1 3.31 us: body(): other = jnp.sum(jnp.where(chosen, piece.astype(jnp.float32), 0.0), axis=0)]
  transfers between devices with their start and end apart: 4 -> 0, of which waited for: 4 -> 0; matrix products, arithmetic and copies ran while one was open for 5% -> 0% of each run, Pallas kernels for 0% -> 0%
where the time goes in v1:
time: 86.2 us; the launch traced here: 85.5 us
  Pallas kernels  75.9 us (88%)
  local copies, waits for them, and re-layouts  8.92 us (10%)
    pallas_call x1, Pallas kernels, body(): pl.pallas_call(kernel, out_shape=(jax.ShapeDtypeStruct((128, 768), BF16),...  75.9 us
    unnamed x17, local copies, waits for them, and re-layouts  8.92 us

profile of v1, /device:TPU:1, one launch (start us, length us, event | category | flops | bytes accessed | tf_op | source)
XLA Modules:
  0.0 85.5 jit_solution(7588815967301160517)
XLA Ops:
  0.6 0.0 copy-start
  0.6 1.6 %copy-done = bf16[1,128,8192]{2,1,0:T(8,128)(2,1)S(1)} copy-done((bf16[1,128,8192]{2,1,0:T(8,128)(2,1)S(1)}, bf16[1,128,8192]{2,1,0:T(8,128)(2,1)}, u32[]{:S(2)}) %copy-start) | copy-done | bytes 2097176
  2.2 0.0 copy-start.1
  2.2 1.1 %copy-done.1 = bf16[1,512,768]{2,1,0:T(8,128)(2,1)S(1)} copy-done((bf16[1,512,768]{2,1,0:T(8,128)(2,1)S(1)}, bf16[1,512,768]{2,1,0:T(8,128)(2,1)}, u32[]{:S(2)}) %copy-start.1) | copy-done | bytes 786456
  3.4 0.0 copy-start.2
  3.4 0.9 %copy-done.2 = f32[1,512,128]{2,1,0:T(8,128)S(1)} copy-done((f32[1,512,128]{2,1,0:T(8,128)S(1)}, f32[1,512,128]{2,1,0:T(8,128)}, u32[]{:S(2)}) %copy-start.2) | copy-done | bytes 262168
  4.3 0.0 copy-start.3
  4.3 0.9 %copy-done.3 = bf16[1,128,768]{2,1,0:T(8,128)(2,1)S(1)} copy-done((bf16[1,128,768]{2,1,0:T(8,128)(2,1)S(1)}, bf16[1,128,768]{2,1,0:T(8,128)(2,1)}, u32[]{:S(2)}) %copy-start.3) | copy-done | bytes 196632
  5.2 0.0 copy-start.4
  5.2 0.8 copy-done.4
  6.0 0.0 copy-start.5
  6.0 0.7 copy-done.5
  6.7 0.0 copy-start.6
  6.7 0.7 copy-done.6
  7.3 75.9 %shard_map.94 = (bf16[128,768]{1,0:T(8,128)(2,1)S(1)}, bf16[512,768]{1,0:T(8,128)(2,1)S(1)}, f32[512,128]{1,0:T(8,128)S(1)}) custom-call(bf16[128,8192]{1,0:T(8,128)(2,1)S(1)} %bitcast.10, f32[1,8192]{1,0:T(1,128)S(1)} %bitcast.17, bf16[4,128,768]{2,1,0:T(8,128)(2,1)S(1)} %bitcast.12, f32[512,128]{1,0:T(8,128)S(1)} %bitcast.14, ...), custom_call_target="tpu_custom_call" | custom-call | tf_op jit(solution)/shard_map/pallas_call | solution.py:331
  83.2 0.7 copy.13
  83.9 0.9 %copy.14 = bf16[1,512,768]{2,1,0:T(8,128)(2,1)} copy(bf16[1,512,768]{2,1,0:T(8,128)(2,1)S(1)} %bitcast.11) | data formatting | bytes 1572864
  84.8 0.7 copy.15
Async XLA Ops:
  0.6 1.6 %copy-start = (bf16[1,128,8192]{2,1,0:T(8,128)(2,1)S(1)}, bf16[1,128,8192]{2,1,0:T(8,128)(2,1)}, u32[]{:S(2)}) copy-start(bf16[1,128,8192]{2,1,0:T(8,128)(2,1)} %param.7) | copy-start | bytes 6291460
  2.2 1.1 %copy-start.1 = (bf16[1,512,768]{2,1,0:T(8,128)(2,1)S(1)}, bf16[1,512,768]{2,1,0:T(8,128)(2,1)}, u32[]{:S(2)}) copy-start(bf16[1,512,768]{2,1,0:T(8,128)(2,1)} %param.9) | copy-start | bytes 2359300
  3.4 0.9 %copy-start.2 = (f32[1,512,128]{2,1,0:T(8,128)S(1)}, f32[1,512,128]{2,1,0:T(8,128)}, u32[]{:S(2)}) copy-start(f32[1,512,128]{2,1,0:T(8,128)} %param.10) | copy-start | bytes 786436
  4.3 0.9 %copy-start.3 = (bf16[1,128,768]{2,1,0:T(8,128)(2,1)S(1)}, bf16[1,128,768]{2,1,0:T(8,128)(2,1)}, u32[]{:S(2)}) copy-start(bf16[1,128,768]{2,1,0:T(8,128)(2,1)} %param.11) | copy-start | bytes 589828
  5.2 0.8 copy-start.4
  6.0 0.7 copy-start.5
  6.7 0.7 copy-start.6

commit v2 on v1

v2 whole, which is shorter than its diff:
```python
import jax
import jax.numpy as jnp
from jax import lax
from jax.experimental import pallas as pl
from jax.experimental.pallas import tpu as pltpu
from jax.sharding import PartitionSpec as P

HD = 128
NC = 4
NA = 2
MESH = pl.DeviceIdType.MESH
F32 = jnp.float32
BF16 = jnp.bfloat16

inner_rate = 0.0001
outer_rate = 0.7
beta_value = 0.9


def kernel(
    tokens, gain_h, weight, momentum, cot, fragment_h, partner_h,
    keys_o, nw_o, nm_o,
    tok, scale, S, R, W2, Cl, Cf, Ca, Cb, Gtf, Gta, Gtb, Gsf, Gsa, Gsb, Grf, Gra, Grb, Pacc, Ps, Pr, Ss, Sr,
    D, X1, X2s, X2r, mom, fragv, gain, fragment, partner_row, partner, keys_v, nw_v, nm_v,
    lsem, a_s, a_r, w_s, w_r, c_s, c_r, f_s, f_r, g_s, g_r, p_s, p_r, k_s, k_r, x1_s, x1_r, x2_s, x2_r,
):
    r = lax.axis_index("replica")
    f = lax.axis_index("fsdp")
    xh = f // 8
    q = f % 8
    y = q // 2
    c = q % 2
    z = r // 2
    C = (Cf, Ca, Cb)
    Gt = (Gtf, Gta, Gtb)
    Gs = (Gsf, Gsa, Gsb)
    Gr = (Grf, Gra, Grb)

    def dev(q2):
        return (r, xh * 8 + q2)

    xpart = (r, (1 - xh) * 8 + q)
    sib = dev(y * 2 + 1 - c)

    small = [
        pltpu.make_async_copy(a, b, lsem.at[n])
        for n, (a, b) in enumerate(((fragment_h, fragment), (partner_h, partner_row), (partner_h, partner), (gain_h, gain)))
    ]
    c_cp = pltpu.make_async_copy(cot, Cl, lsem.at[4])
    w_cp = pltpu.make_async_copy(weight, W2.at[:, xh], lsem.at[5])
    m_cp = pltpu.make_async_copy(momentum, mom, lsem.at[6])
    tok_cp = [
        pltpu.make_async_copy(tokens.at[pl.ds(h * 32, 32)], tok.at[pl.ds(h * 32, 32)], lsem.at[7 + h])
        for h in range(4)
    ]
    for cp in [*small, c_cp, *tok_cp, w_cp, m_cp]:
        cp.start()

    bar = pltpu.get_barrier_semaphore()
    for k in range(1, 8):
        pl.semaphore_signal(bar, inc=1, device_id=dev((q + k) % 8), device_id_type=MESH)
    pl.semaphore_signal(bar, inc=1, device_id=xpart, device_id_type=MESH)

    def greet(k, _):
        pl.semaphore_signal(bar, inc=1, device_id=((r + k) % 32, f), device_id_type=MESH)
        return 0

    lax.fori_loop(1, 32, greet, 0)

    for cp in small:
        cp.wait()
    lane = lax.broadcasted_iota(jnp.int32, (8, 32), 1).astype(F32)
    mine = r.astype(F32)
    partners = jnp.broadcast_to(partner_row[...].astype(F32), (8, 32))
    mate = jnp.sum(jnp.where(lane == mine, partners, 0.0), axis=-1, keepdims=True)
    fragments = jnp.broadcast_to(fragment[...].astype(F32), (8, 32))
    frag_at = jnp.sum(jnp.where(lane == jnp.minimum(mate, mine), fragments, 0.0), axis=-1, keepdims=True)
    fragv[...] = jnp.broadcast_to(frag_at, (8, HD))

    c_cp.wait()
    frag = jnp.broadcast_to(fragv[0:1, :], (128, HD))
    blocks = [Cl[:, j * HD:(j + 1) * HD].astype(F32) for j in range(6)]
    cut = blocks[0]
    for j in range(1, 6):
        cut = jnp.where(frag == float(j), blocks[j], cut)
    Cf[q] = cut.astype(BF16)
    for m in range(5):
        rest = jnp.where(frag <= float(m), blocks[m + 1], blocks[m]).astype(BF16)
        if m < NA:
            Ca[q, :, m * HD:(m + 1) * HD] = rest
        else:
            Cb[q, :, (m - NA) * HD:(m - NA + 1) * HD] = rest

    for cp in tok_cp:
        cp.wait()

    def rows(t, _):
        here = pl.ds(pl.multiple_of(t * 16, 16), 16)
        v = tok[here, :].astype(F32)
        m = jnp.sum(v * v, axis=-1, keepdims=True) * (1.0 / 8192)
        scale[here, :] = jnp.broadcast_to(lax.rsqrt(m + 1e-05), (16, 128))
        return 0

    lax.fori_loop(0, 8, rows, 0)

    def a_send(i, k):
        q2 = (q + k) % 8
        return pltpu.make_async_remote_copy(
            src_ref=S.at[i, q2], dst_ref=R.at[i, q], send_sem=a_s.at[i, k], recv_sem=a_r.at[i, k], device_id=dev(q2),
            device_id_type=MESH)

    def norm_chunk(i):
        def one(b, _):
            for h in range(2):
                col = pl.multiple_of(h * 4096 + b * 512 + i * 128, 128)
                v = tok[:, pl.ds(col, 128)].astype(F32)
                S[i, b, :, h * 128:(h + 1) * 128] = (v * scale[...] * gain[:, pl.ds(col, 128)]).astype(BF16)
            return 0

        lax.fori_loop(0, 8, one, 0)
        R[i, q] = S[i, q]

    def send_chunk(i):
        def one(k, _):
            a_send(i, k).start()
            return 0

        lax.fori_loop(1, 8, one, 0)

    def c_send(g, k):
        to = sib if k == 0 else dev(((y + k) % 4) * 2 + c)
        return pltpu.make_async_remote_copy(
            src_ref=C[g].at[q], dst_ref=C[g].at[q], send_sem=c_s.at[g, k], recv_sem=c_r.at[g, k], device_id=to,
            device_id_type=MESH)

    def c_pass(g, k):
        slot = ((y + 4 - k) % 4) * 2 + c
        return pltpu.make_async_remote_copy(
            src_ref=C[g].at[slot], dst_ref=C[g].at[slot], send_sem=f_s.at[g, k], recv_sem=f_r.at[g, k], device_id=sib,
            device_id_type=MESH)

    def spread(g):
        for k in (2, 1, 3, 0):
            c_send(g, k).start()

    def collect(g):
        for k in (1, 3, 2):
            c_send(g, k).wait_recv()
            c_pass(g, k).start()
        c_send(g, 0).wait_recv()
        for k in (1, 3, 2):
            c_pass(g, k).wait_recv()

    def w_send(i):
        return pltpu.make_async_remote_copy(
            src_ref=W2.at[i, xh], dst_ref=W2.at[i, xh], send_sem=w_s.at[i], recv_sem=w_r.at[i], device_id=xpart,
            device_id_type=MESH)

    norm_chunk(0)
    w_cp.wait()
    pl.semaphore_wait(bar, 39)

    spread(0)
    send_chunk(0)
    for i in range(NC):
        w_send(i).start()
    norm_chunk(1)
    send_chunk(1)
    norm_chunk(2)
    norm_chunk(3)
    collect(0)

    def g_send(g, i):
        return pltpu.make_async_remote_copy(
            src_ref=Gs[g].at[i], dst_ref=Gr[g].at[i], send_sem=g_s.at[g, i], recv_sem=g_r.at[g, i], device_id=xpart,
            device_id_type=MESH)

    def grads(g, i):
        lhs = R[i].reshape(1024, 256)
        width = C[g].shape[-1]
        for n in range(0, width, 256):
            cols = slice(n, min(n + 256, width))
            wide = cols.stop - cols.start
            d = lax.dot_general(
                lhs, C[g][:, :, cols].reshape(1024, wide), (((0,), (0,)), ((), ())), preferred_element_type=F32)
            Gt[g][i, :, :, cols] = d.reshape(2, 128, wide)
        Gs[g][i] = Gt[g][i, 1 - xh].astype(BF16)
        g_send(g, i).start()

    def x1_send(i, k):
        j = (((1 - i // 2) * 8 + (1 - i % 2) + 2 * (k // 2) + 11) % 16) * 2 + k % 2
        return j, pltpu.make_async_remote_copy(
            src_ref=D.at[i, k], dst_ref=X1.at[r], send_sem=x1_s, recv_sem=x1_r, device_id=(j, f), device_id_type=MESH)

    def offer(i):
        g_send(0, i).wait_recv()
        d = inner_rate * (Gtf[i, xh] + Grf[i].astype(F32))
        D[i] = d.astype(BF16).reshape(8, 16, HD)

        def one(k, _):
            j, cp = x1_send(i, k)

            @pl.when(j != r)
            def _():
                cp.start()

            @pl.when(j == r)
            def _():
                X1[r] = D[i, k]

            return 0

        lax.fori_loop(0, 8, one, 0)

    ring_at = (z + 5) % 16
    my_chunk = (1 - ring_at // 8) * 2 + (1 - ring_at % 2)
    my_piece = 2 * ((ring_at % 8) // 2) + r % 2

    def x2_send(k):
        d = (r + k) % 32
        return pltpu.make_async_remote_copy(
            src_ref=X2s.at[d], dst_ref=X2r.at[my_chunk, my_piece], send_sem=x2_s, recv_sem=x2_r.at[my_chunk],
            device_id=(d, f), device_id_type=MESH)

    def relay():
        whole = X1.at[pl.ds(0, 31)]
        pltpu.make_async_copy(whole, whole, x1_r).wait()

        def pick(d, _):
            X2s[d] = X1[partner[0, d]]
            return 0

        lax.fori_loop(0, 32, pick, 0)

        def one(k, _):
            x2_send(k).start()
            return 0

        lax.fori_loop(1, 32, one, 0)
        X2r[my_chunk, my_piece] = X2s[r]

    def step(t, _):
        def arrive(k, _):
            a_send(t, k).wait_recv()
            return 0

        lax.fori_loop(1, 8, arrive, 0)

        @pl.when(t == 0)
        def _():
            send_chunk(2)

        @pl.when(t == 1)
        def _():
            spread(1)
            send_chunk(3)

        grads(0, t)

        w_send(t).wait_recv()

        @pl.when(t == 0)
        def _():
            Pacc[...] = jnp.zeros_like(Pacc)

        lhs = R[t].reshape(1024, 256)
        for n in range(3):
            cols = slice(n * 256, (n + 1) * 256)
            p = jnp.dot(lhs, W2[t, :, :, cols].reshape(256, 256), preferred_element_type=F32)
            Pacc[:, :, cols] += p.reshape(8, 128, 256)

        @pl.when(t >= 1)
        def _():
            offer(t - 1)

        @pl.when(t == 2)
        def _():
            spread(2)
            collect(1)

            def early(i, _):
                grads(1, i)
                return 0

            lax.fori_loop(0, NC - 1, early, 0)

        return 0

    lax.fori_loop(0, NC, step, 0)

    p_send = pltpu.make_async_remote_copy(
        src_ref=Ps, dst_ref=Pr, send_sem=p_s, recv_sem=p_r, device_id=sib, device_id_type=MESH)
    for b in range(4):
        Ps[b] = Pacc[b * 2 + 1 - c].astype(BF16)
    p_send.start()
    offer(NC - 1)
    grads(1, NC - 1)

    @pl.when(my_chunk < 2)
    def _():
        relay()

    def k_send(k):
        y2 = (y + k) % 4
        return pltpu.make_async_remote_copy(
            src_ref=Ss.at[y2], dst_ref=Sr.at[k - 1], send_sem=k_s.at[k], recv_sem=k_r.at[k], device_id=dev(y2 * 2 + c),
            device_id_type=MESH)

    p_send.wait_recv()
    for k in (2, 1, 3):
        y2 = (y + k) % 4
        Ss[y2] = (Pacc[y2 * 2 + c] + Pr[y2].astype(F32)).astype(BF16)
        k_send(k).start()

    collect(2)

    def late(i, _):
        grads(2, i)
        return 0

    lax.fori_loop(0, NC, late, 0)

    @pl.when(my_chunk >= 2)
    def _():
        relay()

    for k in (1, 3, 2):
        k_send(k).wait_recv()
    own = Pacc[q] + Pr[y].astype(F32)
    keys_v[...] = (own + Sr[0].astype(F32) + Sr[1].astype(F32) + Sr[2].astype(F32)).astype(BF16)
    keys_cp = pltpu.make_async_copy(keys_v, keys_o, lsem.at[11])
    keys_cp.start()

    m_cp.wait()

    def add_up(i, _):
        g_send(1, i).wait_recv()
        g_send(2, i).wait_recv()
        Gta[i, xh] = Gta[i, xh] + Gra[i].astype(F32)
        Gtb[i, xh] = Gtb[i, xh] + Grb[i].astype(F32)
        return 0

    lax.fori_loop(0, NC, add_up, 0)

    def update(i, _):
        @pl.when(my_chunk == i)
        def _():
            part = X2r.at[i, pl.ds(0, 7)]
            pltpu.make_async_copy(part, part, x2_r.at[i]).wait()

        @pl.when(my_chunk != i)
        def _():
            part = X2r.at[i]
            pltpu.make_async_copy(part, part, x2_r.at[i]).wait()

        here = pl.ds(pl.multiple_of(i * 128, 128), 128)
        delta = D[i].reshape(128, HD).astype(F32)
        mix = (delta + X2r[i].reshape(128, HD).astype(F32)) * 0.5
        nm = beta_value * mom[here, :] + mix
        nm_v[here, :] = nm
        step_out = outer_rate * (beta_value * nm + mix)
        at = jnp.broadcast_to(fragv[0:1, :], (128, HD))

        def rest(m):
            if m < NA:
                return Gta[i, xh, :, m * HD:(m + 1) * HD]
            return Gtb[i, xh, :, (m - NA) * HD:(m - NA + 1) * HD]

        for j in range(6):
            cols = slice(j * HD, (j + 1) * HD)
            if j == 0:
                g = rest(0)
            elif j == 5:
                g = rest(4)
            else:
                g = jnp.where(at < float(j), rest(j - 1), rest(j))
            change = jnp.where(at == float(j), step_out, inner_rate * g)
            nw_v[here, cols] = (W2[i, xh, :, cols].astype(F32) - change).astype(BF16)
        return 0

    lax.fori_loop(0, NC, update, 0)
    nw_cp = pltpu.make_async_copy(nw_v, nw_o, lsem.at[12])
    nw_cp.start()
    nm_cp = pltpu.make_async_copy(nm_v, nm_o, lsem.at[13])
    nm_cp.start()

    for k in range(4):
        for g in range(3):
            c_send(g, k).wait_send()
            if k > 0:
                c_pass(g, k).wait_send()
        if k > 0:
            k_send(k).wait_send()
    p_send.wait_send()

    def sent(i, _):
        w_send(i).wait_send()
        for g in range(3):
            g_send(g, i).wait_send()

        def one(k, _):
            a_send(i, k).wait_send()
            return 0

        lax.fori_loop(1, 8, one, 0)
        return 0

    lax.fori_loop(0, NC, sent, 0)
    most = X1.at[pl.ds(0, 31)]
    pltpu.make_async_copy(most, most, x1_s).wait()
    pltpu.make_async_copy(most, most, x2_s).wait()
    for cp in (keys_cp, nw_cp, nm_cp):
        cp.wait()


def finish(keys, nw, nm, keys_o, nw_o, nm_o, keys_v, nw_v, nm_v, i_sem, o_sem):
    ways = [(nw.at[here], nw_v.at[here], nw_o.at[here]) for here in (pl.ds(0, 256), pl.ds(256, 256))]
    ways += [(nm, nm_v, nm_o), (keys, keys_v, keys_o)]
    into = [pltpu.make_async_copy(a, v, i_sem.at[n]) for n, (a, v, _) in enumerate(ways)]
    out = [pltpu.make_async_copy(v, b, o_sem.at[n]) for n, (_, v, b) in enumerate(ways)]
    for cp in into:
        cp.start()
    for cp, back in zip(into, out):
        cp.wait()
        back.start()
    for back in out:
        back.wait()


def body(tokens, norm_gain, weight, momentum, cotangent, fragment, partner):
    hbm = pl.BlockSpec(memory_space=pltpu.HBM)
    V = pltpu.VMEM
    dma = pltpu.SemaphoreType.DMA
    shapes = (
        jax.ShapeDtypeStruct((128, 768), BF16),
        jax.ShapeDtypeStruct((512, 768), BF16),
        jax.ShapeDtypeStruct((512, HD), F32),
    )
    na, nb = NA * HD, (5 - NA) * HD
    outs = pl.pallas_call(
        kernel,
        out_shape=shapes,
        in_specs=[hbm] * 7,
        out_specs=(hbm,) * 3,
        scratch_shapes=[
            V((128, 8192), BF16),
            V((128, 128), F32),
            V((NC, 8, 128, 256), BF16),
            V((NC, 8, 128, 256), BF16),
            V((NC, 2, 128, 768), BF16),
            V((128, 768), BF16),
            V((8, 128, HD), BF16), V((8, 128, na), BF16), V((8, 128, nb), BF16),
            V((NC, 2, 128, HD), F32), V((NC, 2, 128, na), F32), V((NC, 2, 128, nb), F32),
            V((NC, 128, HD), BF16), V((NC, 128, na), BF16), V((NC, 128, nb), BF16),
            V((NC, 128, HD), BF16), V((NC, 128, na), BF16), V((NC, 128, nb), BF16),
            V((8, 128, 768), F32),
            V((4, 128, 768), BF16),
            V((4, 128, 768), BF16),
            V((4, 128, 768), BF16),
            V((3, 128, 768), BF16),
            V((NC, 8, 16, HD), BF16),
            V((32, 16, HD), BF16),
            V((32, 16, HD), BF16),
            V((NC, 8, 16, HD), BF16),
            V((512, HD), F32),
            V((8, HD), F32),
            V((1, 8192), F32),
            V((1, 32), jnp.int32),
            V((1, 32), jnp.int32),
            pltpu.SMEM((1, 32), jnp.int32),
            V((128, 768), BF16), V((512, 768), BF16), V((512, HD), F32),
            dma((14,)),
            dma((NC, 8)), dma((NC, 8)),
            dma((NC,)), dma((NC,)),
            dma((3, 4)), dma((3, 4)),
            dma((3, 4)), dma((3, 4)),
            dma((3, NC)), dma((3, NC)),
            dma, dma,
            dma((4,)), dma((4,)),
            dma, dma,
            dma, dma((NC,)),
        ],
        compiler_params=pltpu.CompilerParams(
            collective_id=0, has_side_effects=True, vmem_limit_bytes=62 * 2**20
        ),
    )(tokens[0], norm_gain[None], weight[0].reshape(NC, 128, 768), momentum[0], cotangent[0], fragment[None], partner[None])
    keys, nw, nm = pl.pallas_call(
        finish,
        out_shape=shapes,
        in_specs=[hbm] * 3,
        out_specs=(hbm,) * 3,
        scratch_shapes=[V((128, 768), BF16), V((512, 768), BF16), V((512, HD), F32), dma((4,)), dma((4,))],
        compiler_params=pltpu.CompilerParams(vmem_limit_bytes=62 * 2**20),
    )(*outs)
    return (keys[None], nw[None], nm[None])


def solution(mesh):
    in_specs = (
        P("replica", "fsdp", None),
        P(),
        P("replica", "fsdp", None),
        P("replica", "fsdp", None),
        P("replica", "fsdp", None),
        P(),
        P(),
    )
    out_specs = (P("replica", "fsdp", None), P("replica", "fsdp", None), P("replica", "fsdp", None))
    return jax.shard_map(body, mesh=mesh, in_specs=in_specs, out_specs=out_specs, check_vma=False)
```

time: 86.2 us -> 74.1 us (0.86)
  the two profiles are of different devices: /device:TPU:1 before, /device:TPU:8 now
where the time goes in v2:
time: 74.1 us; the launch traced here: 73.9 us
  Pallas kernels  73.3 us (99%)
    pallas_call x1, Pallas kernels, body(): pl.pallas_call(kernel, out_shape=shapes, in_specs=[hbm] * 7, out_specs=(h...  71.2 us
    pallas_call x1, Pallas kernels, body(): pl.pallas_call(finish, out_shape=shapes, in_specs=[hbm] * 3, out_specs=(h...  2.09 us

profile of v2, /device:TPU:8, one launch (start us, length us, event | category | flops | bytes accessed | tf_op | source)
XLA Modules:
  0.0 73.9 jit_solution(10547325718111633204)
XLA Ops:
  0.6 71.2 %shard_map.94 = (bf16[128,768]{1,0:T(8,128)(2,1)}, bf16[512,768]{1,0:T(8,128)(2,1)}, f32[512,128]{1,0:T(8,128)}) custom-call(bf16[128,8192]{1,0:T(8,128)(2,1)} %bitcast.10, f32[1,8192]{1,0:T(1,128)} %bitcast.14, bf16[4,128,768]{2,1,0:T(8,128)(2,1)} %bitcast.11, f32[512,128]{1,0:T(8,128)} %bitcast.12, bf16[128,768]{1,0:T(8,128)(2,1)} %bitcast.13, ...), custom_call_target="tpu_custom_call" | custom-call | tf_op jit(solution)/shard_map/pallas_call | solution.py:440
  71.8 2.1 %shard_map.95 = (bf16[128,768]{1,0:T(8,128)(2,1)}, bf16[512,768]{1,0:T(8,128)(2,1)}, f32[512,128]{1,0:T(8,128)}) custom-call(bf16[128,768]{1,0:T(8,128)(2,1)} %get-tuple-element.9.keys, bf16[512,768]{1,0:T(8,128)(2,1)} %get-tuple-element.10.nw, f32[512,128]{1,0:T(8,128)} %get-tuple-element.11.nm), custom_call_target="tpu_custom_call" | custom-call | tf_op jit(solution)/shard_map/pallas_call | solution.py:487

commit v3 on v2

--- a/solution.py
+++ b/solution.py
@@ -22,7 +22,7 @@
     keys_o, nw_o, nm_o,
     tok, scale, S, R, W2, Cl, Cf, Ca, Cb, Gtf, Gta, Gtb, Gsf, Gsa, Gsb, Grf, Gra, Grb, Pacc, Ps, Pr, Ss, Sr,
     D, X1, X2s, X2r, mom, fragv, gain, fragment, partner_row, partner, keys_v, nw_v, nm_v,
-    lsem, a_s, a_r, w_s, w_r, c_s, c_r, f_s, f_r, g_s, g_r, p_s, p_r, k_s, k_r, x1_s, x1_r, x2_s, x2_r,
+    lsem, a_s, a_r, w_s, w_r, c_s, c_r, f_s, f_r, g_s, g_r, p_s, p_r, k_s, k_r, x1_s, x1_r, x2_s, x2_r, near,
 ):
     r = lax.axis_index("replica")
     f = lax.axis_index("fsdp")
@@ -61,11 +61,27 @@
         pl.semaphore_signal(bar, inc=1, device_id=dev((q + k) % 8), device_id_type=MESH)
     pl.semaphore_signal(bar, inc=1, device_id=xpart, device_id_type=MESH)
 
-    def greet(k, _):
-        pl.semaphore_signal(bar, inc=1, device_id=((r + k) % 32, f), device_id_type=MESH)
-        return 0
-
-    lax.fori_loop(1, 32, greet, 0)
+    pl.semaphore_signal(bar, inc=1, device_id=(z * 2 + 1 - r % 2, f), device_id_type=MESH)
+
+    def in_line(away):
+        return (z + away >= 0) & (z + away < 16)
+
+    for away in (-1, 1):
+        @pl.when(in_line(away))
+        def _():
+            for h in range(2):
+                pl.semaphore_signal(bar, inc=1, device_id=((z + away) * 2 + h, f), device_id_type=MESH)
+
+    def tell(level):
+        far = 2 ** level
+        for away in (-far, far):
+            @pl.when(in_line(away))
+            def _():
+                pl.semaphore_signal(near.at[level], inc=1, device_id=(r + 2 * away, f), device_id_type=MESH)
+
+    def hear(level):
+        far = 2 ** level
+        pl.semaphore_wait(near.at[level], jnp.minimum(z // far, 1) + jnp.minimum((15 - z) // far, 1))
 
     for cp in small:
         cp.wait()
@@ -158,7 +174,7 @@
 
     norm_chunk(0)
     w_cp.wait()
-    pl.semaphore_wait(bar, 39)
+    pl.semaphore_wait(bar, 9 + 2 * jnp.minimum(z, 1) + 2 * jnp.minimum(15 - z, 1))
 
     spread(0)
     send_chunk(0)
@@ -166,9 +182,12 @@
         w_send(i).start()
     norm_chunk(1)
     send_chunk(1)
+    tell(0)
     norm_chunk(2)
     norm_chunk(3)
     collect(0)
+    hear(0)
+    tell(1)
 
     def g_send(g, i):
         return pltpu.make_async_remote_copy(
@@ -248,11 +267,11 @@
 
         @pl.when(t == 0)
         def _():
+            spread(1)
             send_chunk(2)
 
         @pl.when(t == 1)
         def _():
-            spread(1)
             send_chunk(3)
 
         grads(0, t)
@@ -269,9 +288,15 @@
             p = jnp.dot(lhs, W2[t, :, :, cols].reshape(256, 256), preferred_element_type=F32)
             Pacc[:, :, cols] += p.reshape(8, 128, 256)
 
-        @pl.when(t >= 1)
-        def _():
-            offer(t - 1)
+        @pl.when(t == 0)
+        def _():
+            hear(1)
+            tell(2)
+
+        @pl.when(t == 1)
+        def _():
+            hear(2)
+            tell(3)
 
         @pl.when(t == 2)
         def _():
@@ -293,7 +318,13 @@
     for b in range(4):
         Ps[b] = Pacc[b * 2 + 1 - c].astype(BF16)
     p_send.start()
-    offer(NC - 1)
+    hear(3)
+
+    def offers(i, _):
+        offer(i)
+        return 0
+
+    lax.fori_loop(0, NC, offers, 0)
     grads(1, NC - 1)
 
     @pl.when(my_chunk < 2)
@@ -479,6 +510,7 @@
             dma((4,)), dma((4,)),
             dma, dma,
             dma, dma((NC,)),
+            pltpu.SemaphoreType.REGULAR((4,)),
         ],
         compiler_params=pltpu.CompilerParams(
             collective_id=0, has_side_effects=True, vmem_limit_bytes=62 * 2**20

time: 74.1 us -> 73.2 us (0.988)
  the two profiles are of different devices: /device:TPU:8 before, /device:TPU:96 now
where the time goes in v3:
time: 73.2 us; the launch traced here: 73 us
  Pallas kernels  72.4 us (99%)
    pallas_call x1, Pallas kernels, body(): pl.pallas_call(kernel, out_shape=shapes, in_specs=[hbm] * 7, out_specs=(h...  70.3 us
    pallas_call x1, Pallas kernels, body(): pl.pallas_call(finish, out_shape=shapes, in_specs=[hbm] * 3, out_specs=(h...  2.09 us

profile of v3, /device:TPU:96, one launch (start us, length us, event | category | flops | bytes accessed | tf_op | source)
XLA Modules:
  0.0 73.0 jit_solution(3166282853858379817)
XLA Ops:
  0.6 70.3 %shard_map.94 = (bf16[128,768]{1,0:T(8,128)(2,1)}, bf16[512,768]{1,0:T(8,128)(2,1)}, f32[512,128]{1,0:T(8,128)}) custom-call(bf16[128,8192]{1,0:T(8,128)(2,1)} %bitcast.10, f32[1,8192]{1,0:T(1,128)} %bitcast.14, bf16[4,128,768]{2,1,0:T(8,128)(2,1)} %bitcast.11, f32[512,128]{1,0:T(8,128)} %bitcast.12, bf16[128,768]{1,0:T(8,128)(2,1)} %bitcast.13, ...), custom_call_target="tpu_custom_call" | custom-call | tf_op jit(solution)/shard_map/pallas_call | solution.py:471
  70.9 2.1 %shard_map.95 = (bf16[128,768]{1,0:T(8,128)(2,1)}, bf16[512,768]{1,0:T(8,128)(2,1)}, f32[512,128]{1,0:T(8,128)}) custom-call(bf16[128,768]{1,0:T(8,128)(2,1)} %get-tuple-element.9.keys, bf16[512,768]{1,0:T(8,128)(2,1)} %get-tuple-element.10.nw, f32[512,128]{1,0:T(8,128)} %get-tuple-element.11.nm), custom_call_target="tpu_custom_call" | custom-call | tf_op jit(solution)/shard_map/pallas_call | solution.py:519

commit v4 on v3

--- a/solution.py
+++ b/solution.py
@@ -22,7 +22,7 @@
     keys_o, nw_o, nm_o,
     tok, scale, S, R, W2, Cl, Cf, Ca, Cb, Gtf, Gta, Gtb, Gsf, Gsa, Gsb, Grf, Gra, Grb, Pacc, Ps, Pr, Ss, Sr,
     D, X1, X2s, X2r, mom, fragv, gain, fragment, partner_row, partner, keys_v, nw_v, nm_v,
-    lsem, a_s, a_r, w_s, w_r, c_s, c_r, f_s, f_r, g_s, g_r, p_s, p_r, k_s, k_r, x1_s, x1_r, x2_s, x2_r, near,
+    lsem, a_s, a_r, w_s, w_r, c_s, c_r, f_s, f_r, g_s, g_r, p_s, p_r, k_s, k_r, x1_s, x1_r, x2_s, x2_r, near, o_sem,
 ):
     r = lax.axis_index("replica")
     f = lax.axis_index("fsdp")
@@ -107,9 +107,6 @@
         else:
             Cb[q, :, (m - NA) * HD:(m - NA + 1) * HD] = rest
 
-    for cp in tok_cp:
-        cp.wait()
-
     def rows(t, _):
         here = pl.ds(pl.multiple_of(t * 16, 16), 16)
         v = tok[here, :].astype(F32)
@@ -117,7 +114,9 @@
         scale[here, :] = jnp.broadcast_to(lax.rsqrt(m + 1e-05), (16, 128))
         return 0
 
-    lax.fori_loop(0, 8, rows, 0)
+    for h, cp in enumerate(tok_cp):
+        cp.wait()
+        lax.fori_loop(2 * h, 2 * h + 2, rows, 0)
 
     def a_send(i, k):
         q2 = (q + k) % 8
@@ -231,12 +230,18 @@
 
         lax.fori_loop(0, 8, one, 0)
 
+    def offers(first, last):
+        def one(i, _):
+            offer(i)
+            return 0
+
+        lax.fori_loop(first, last, one, 0)
+
     ring_at = (z + 5) % 16
     my_chunk = (1 - ring_at // 8) * 2 + (1 - ring_at % 2)
     my_piece = 2 * ((ring_at % 8) // 2) + r % 2
 
-    def x2_send(k):
-        d = (r + k) % 32
+    def x2_send(d):
         return pltpu.make_async_remote_copy(
             src_ref=X2s.at[d], dst_ref=X2r.at[my_chunk, my_piece], send_sem=x2_s, recv_sem=x2_r.at[my_chunk],
             device_id=(d, f), device_id_type=MESH)
@@ -245,17 +250,16 @@
         whole = X1.at[pl.ds(0, 31)]
         pltpu.make_async_copy(whole, whole, x1_r).wait()
 
-        def pick(d, _):
+        def one(d, _):
             X2s[d] = X1[partner[0, d]]
-            return 0
-
-        lax.fori_loop(0, 32, pick, 0)
-
-        def one(k, _):
-            x2_send(k).start()
-            return 0
-
-        lax.fori_loop(1, 32, one, 0)
+
+            @pl.when(d != r)
+            def _():
+                x2_send(d).start()
+
+            return 0
+
+        lax.fori_loop(0, 32, one, 0)
         X2r[my_chunk, my_piece] = X2s[r]
 
     def step(t, _):
@@ -308,6 +312,8 @@
                 return 0
 
             lax.fori_loop(0, NC - 1, early, 0)
+            hear(3)
+            offers(0, NC - 2)
 
         return 0
 
@@ -318,18 +324,8 @@
     for b in range(4):
         Ps[b] = Pacc[b * 2 + 1 - c].astype(BF16)
     p_send.start()
-    hear(3)
-
-    def offers(i, _):
-        offer(i)
-        return 0
-
-    lax.fori_loop(0, NC, offers, 0)
+    offers(NC - 2, NC)
     grads(1, NC - 1)
-
-    @pl.when(my_chunk < 2)
-    def _():
-        relay()
 
     def k_send(k):
         y2 = (y + k) % 4
@@ -351,9 +347,7 @@
 
     lax.fori_loop(0, NC, late, 0)
 
-    @pl.when(my_chunk >= 2)
-    def _():
-        relay()
+    relay()
 
     for k in (1, 3, 2):
         k_send(k).wait_recv()
@@ -364,14 +358,37 @@
 
     m_cp.wait()
 
-    def add_up(i, _):
+    def inner(i, _):
         g_send(1, i).wait_recv()
         g_send(2, i).wait_recv()
-        Gta[i, xh] = Gta[i, xh] + Gra[i].astype(F32)
-        Gtb[i, xh] = Gtb[i, xh] + Grb[i].astype(F32)
-        return 0
-
-    lax.fori_loop(0, NC, add_up, 0)
+        here = pl.ds(pl.multiple_of(i * 128, 128), 128)
+        at = jnp.broadcast_to(fragv[0:1, :], (128, HD))
+
+        def rest(m):
+            g, n = (1, m) if m < NA else (2, m - NA)
+            cols = slice(n * HD, (n + 1) * HD)
+            return Gt[g][i, xh, :, cols] + Gr[g][i, :, cols].astype(F32)
+
+        grads_of = [rest(m) for m in range(5)]
+        for j in range(6):
+            if j == 0:
+                g = grads_of[0]
+            elif j == 5:
+                g = grads_of[4]
+            else:
+                g = jnp.where(at < float(j), grads_of[j - 1], grads_of[j])
+            cols = slice(j * HD, (j + 1) * HD)
+            nw_v[here, cols] = (W2[i, xh, :, cols].astype(F32) - inner_rate * g).astype(BF16)
+        return 0
+
+    lax.fori_loop(0, NC, inner, 0)
+
+    def out_copies(i):
+        here = pl.ds(pl.multiple_of(i * 128, 128), 128)
+        return (
+            pltpu.make_async_copy(nw_v.at[here], nw_o.at[here], o_sem.at[0, i]),
+            pltpu.make_async_copy(nm_v.at[here], nm_o.at[here], o_sem.at[1, i]),
+        )
 
     def update(i, _):
         @pl.when(my_chunk == i)
@@ -391,29 +408,15 @@
         nm_v[here, :] = nm
         step_out = outer_rate * (beta_value * nm + mix)
         at = jnp.broadcast_to(fragv[0:1, :], (128, HD))
-
-        def rest(m):
-            if m < NA:
-                return Gta[i, xh, :, m * HD:(m + 1) * HD]
-            return Gtb[i, xh, :, (m - NA) * HD:(m - NA + 1) * HD]
-
         for j in range(6):
             cols = slice(j * HD, (j + 1) * HD)
-            if j == 0:
-                g = rest(0)
-            elif j == 5:
-                g = rest(4)
-            else:
-                g = jnp.where(at < float(j), rest(j - 1), rest(j))
-            change = jnp.where(at == float(j), step_out, inner_rate * g)
-            nw_v[here, cols] = (W2[i, xh, :, cols].astype(F32) - change).astype(BF16)
+            outer = W2[i, xh, :, cols].astype(F32) - step_out
+            nw_v[here, cols] = jnp.where(at == float(j), outer, nw_v[here, cols].astype(F32)).astype(BF16)
+        for cp in out_copies(i):
+            cp.start()
         return 0
 
     lax.fori_loop(0, NC, update, 0)
-    nw_cp = pltpu.make_async_copy(nw_v, nw_o, lsem.at[12])
-    nw_cp.start()
-    nm_cp = pltpu.make_async_copy(nm_v, nm_o, lsem.at[13])
-    nm_cp.start()
 
     for k in range(4):
         for g in range(3):
@@ -440,8 +443,14 @@
     most = X1.at[pl.ds(0, 31)]
     pltpu.make_async_copy(most, most, x1_s).wait()
     pltpu.make_async_copy(most, most, x2_s).wait()
-    for cp in (keys_cp, nw_cp, nm_cp):
-        cp.wait()
+    keys_cp.wait()
+
+    def written(i, _):
+        for cp in out_copies(i):
+            cp.wait()
+        return 0
+
+    lax.fori_loop(0, NC, written, 0)
 
 
 def finish(keys, nw, nm, keys_o, nw_o, nm_o, keys_v, nw_v, nm_v, i_sem, o_sem):
@@ -500,7 +509,7 @@
             V((1, 32), jnp.int32),
             pltpu.SMEM((1, 32), jnp.int32),
             V((128, 768), BF16), V((512, 768), BF16), V((512, HD), F32),
-            dma((14,)),
+            dma((12,)),
             dma((NC, 8)), dma((NC, 8)),
             dma((NC,)), dma((NC,)),
             dma((3, 4)), dma((3, 4)),
@@ -511,6 +520,7 @@
             dma, dma,
             dma, dma((NC,)),
             pltpu.SemaphoreType.REGULAR((4,)),
+            dma((2, NC)),
         ],
         compiler_params=pltpu.CompilerParams(
             collective_id=0, has_side_effects=True, vmem_limit_bytes=62 * 2**20

time: 73.2 us -> 66.8 us (0.913)
  the two profiles are of different devices: /device:TPU:96 before, /device:TPU:1 now
where the time goes in v4:
time: 66.8 us; the launch traced here: 66.7 us
  Pallas kernels  66.1 us (99%)
    pallas_call x1, Pallas kernels, body(): pl.pallas_call(kernel, out_shape=shapes, in_specs=[hbm] * 7, out_specs=(h...  64 us
    pallas_call x1, Pallas kernels, body(): pl.pallas_call(finish, out_shape=shapes, in_specs=[hbm] * 3, out_specs=(h...  2.09 us

profile of v4, /device:TPU:1, one launch (start us, length us, event | category | flops | bytes accessed | tf_op | source)
XLA Modules:
  0.0 66.7 jit_solution(16009697000926962313)
XLA Ops:
  0.6 64.0 %shard_map.94 = (bf16[128,768]{1,0:T(8,128)(2,1)}, bf16[512,768]{1,0:T(8,128)(2,1)}, f32[512,128]{1,0:T(8,128)}) custom-call(bf16[128,8192]{1,0:T(8,128)(2,1)} %bitcast.10, f32[1,8192]{1,0:T(1,128)} %bitcast.14, bf16[4,128,768]{2,1,0:T(8,128)(2,1)} %bitcast.11, f32[512,128]{1,0:T(8,128)} %bitcast.12, bf16[128,768]{1,0:T(8,128)(2,1)} %bitcast.13, ...), custom_call_target="tpu_custom_call" | custom-call | tf_op jit(solution)/shard_map/pallas_call | solution.py:480
  64.6 2.1 %shard_map.95 = (bf16[128,768]{1,0:T(8,128)(2,1)}, bf16[512,768]{1,0:T(8,128)(2,1)}, f32[512,128]{1,0:T(8,128)}) custom-call(bf16[128,768]{1,0:T(8,128)(2,1)} %get-tuple-element.9.keys, bf16[512,768]{1,0:T(8,128)(2,1)} %get-tuple-element.10.nw, f32[512,128]{1,0:T(8,128)} %get-tuple-element.11.nm), custom_call_target="tpu_custom_call" | custom-call | tf_op jit(solution)/shard_map/pallas_call | solution.py:529

commit v5 on v4

--- a/solution.py
+++ b/solution.py
@@ -7,7 +7,7 @@
 
 HD = 128
 NC = 4
-NA = 2
+NA = 1
 MESH = pl.DeviceIdType.MESH
 F32 = jnp.float32
 BF16 = jnp.bfloat16
@@ -206,7 +206,7 @@
         g_send(g, i).start()
 
     def x1_send(i, k):
-        j = (((1 - i // 2) * 8 + (1 - i % 2) + 2 * (k // 2) + 11) % 16) * 2 + k % 2
+        j = ((i // 2) * 8 + 2 * (k // 2) + i % 2) * 2 + k % 2
         return j, pltpu.make_async_remote_copy(
             src_ref=D.at[i, k], dst_ref=X1.at[r], send_sem=x1_s, recv_sem=x1_r, device_id=(j, f), device_id_type=MESH)
 
@@ -237,9 +237,8 @@
 
         lax.fori_loop(first, last, one, 0)
 
-    ring_at = (z + 5) % 16
-    my_chunk = (1 - ring_at // 8) * 2 + (1 - ring_at % 2)
-    my_piece = 2 * ((ring_at % 8) // 2) + r % 2
+    my_chunk = 2 * (z // 8) + z % 2
+    my_piece = 2 * ((z % 8) // 2) + r % 2
 
     def x2_send(d):
         return pltpu.make_async_remote_copy(

time: 66.8 us -> 64.7 us (0.969)
  Pallas kernels: 66.1 us -> 63.6 us
    pallas_call x1, Pallas kernels: 64 us -> 61.5 us  [body(): pl.pallas_call(kernel, out_shape=shapes, in_specs=[hbm] * 7, out_specs=(h...]
where the time goes in v5:
time: 64.7 us; the launch traced here: 64.2 us
  Pallas kernels  63.6 us (98%)
    pallas_call x1, Pallas kernels, body(): pl.pallas_call(kernel, out_shape=shapes, in_specs=[hbm] * 7, out_specs=(h...  61.5 us
    pallas_call x1, Pallas kernels, body(): pl.pallas_call(finish, out_shape=shapes, in_specs=[hbm] * 3, out_specs=(h...  2.09 us

profile of v5, /device:TPU:1, one launch (start us, length us, event | category | flops | bytes accessed | tf_op | source)
XLA Modules:
  0.0 64.2 jit_solution(1528900374373465213)
XLA Ops:
  0.6 61.5 %shard_map.94 = (bf16[128,768]{1,0:T(8,128)(2,1)}, bf16[512,768]{1,0:T(8,128)(2,1)}, f32[512,128]{1,0:T(8,128)}) custom-call(bf16[128,8192]{1,0:T(8,128)(2,1)} %bitcast.10, f32[1,8192]{1,0:T(1,128)} %bitcast.14, bf16[4,128,768]{2,1,0:T(8,128)(2,1)} %bitcast.11, f32[512,128]{1,0:T(8,128)} %bitcast.12, bf16[128,768]{1,0:T(8,128)(2,1)} %bitcast.13, ...), custom_call_target="tpu_custom_call" | custom-call | tf_op jit(solution)/shard_map/pallas_call | solution.py:479
  62.1 2.1 %shard_map.95 = (bf16[128,768]{1,0:T(8,128)(2,1)}, bf16[512,768]{1,0:T(8,128)(2,1)}, f32[512,128]{1,0:T(8,128)}) custom-call(bf16[128,768]{1,0:T(8,128)(2,1)} %get-tuple-element.9.keys, bf16[512,768]{1,0:T(8,128)(2,1)} %get-tuple-element.10.nw, f32[512,128]{1,0:T(8,128)} %get-tuple-element.11.nm), custom_call_target="tpu_custom_call" | custom-call | tf_op jit(solution)/shard_map/pallas_call | solution.py:528

commit v6 on v5

--- a/solution.py
+++ b/solution.py
@@ -382,6 +382,31 @@
 
     lax.fori_loop(0, NC, inner, 0)
 
+    for k in range(4):
+        for g in range(3):
+            c_send(g, k).wait_send()
+            if k > 0:
+                c_pass(g, k).wait_send()
+        if k > 0:
+            k_send(k).wait_send()
+    p_send.wait_send()
+
+    def sent(i, _):
+        w_send(i).wait_send()
+        for g in range(3):
+            g_send(g, i).wait_send()
+
+        def one(k, _):
+            a_send(i, k).wait_send()
+            return 0
+
+        lax.fori_loop(1, 8, one, 0)
+        return 0
+
+    lax.fori_loop(0, NC, sent, 0)
+    most = X1.at[pl.ds(0, 31)]
+    pltpu.make_async_copy(most, most, x1_s).wait()
+
     def out_copies(i):
         here = pl.ds(pl.multiple_of(i * 128, 128), 128)
         return (
@@ -417,30 +442,6 @@
 
     lax.fori_loop(0, NC, update, 0)
 
-    for k in range(4):
-        for g in range(3):
-            c_send(g, k).wait_send()
-            if k > 0:
-                c_pass(g, k).wait_send()
-        if k > 0:
-            k_send(k).wait_send()
-    p_send.wait_send()
-
-    def sent(i, _):
-        w_send(i).wait_send()
-        for g in range(3):
-            g_send(g, i).wait_send()
-
-        def one(k, _):
-            a_send(i, k).wait_send()
-            return 0
-
-        lax.fori_loop(1, 8, one, 0)
-        return 0
-
-    lax.fori_loop(0, NC, sent, 0)
-    most = X1.at[pl.ds(0, 31)]
-    pltpu.make_async_copy(most, most, x1_s).wait()
     pltpu.make_async_copy(most, most, x2_s).wait()
     keys_cp.wait()
 
@@ -453,7 +454,7 @@
 
 
 def finish(keys, nw, nm, keys_o, nw_o, nm_o, keys_v, nw_v, nm_v, i_sem, o_sem):
-    ways = [(nw.at[here], nw_v.at[here], nw_o.at[here]) for here in (pl.ds(0, 256), pl.ds(256, 256))]
+    ways = [(nw.at[here], nw_v.at[here], nw_o.at[here]) for here in (pl.ds(k * 128, 128) for k in range(4))]
     ways += [(nm, nm_v, nm_o), (keys, keys_v, keys_o)]
     into = [pltpu.make_async_copy(a, v, i_sem.at[n]) for n, (a, v, _) in enumerate(ways)]
     out = [pltpu.make_async_copy(v, b, o_sem.at[n]) for n, (_, v, b) in enumerate(ways)]
@@ -530,7 +531,7 @@
         out_shape=shapes,
         in_specs=[hbm] * 3,
         out_specs=(hbm,) * 3,
-        scratch_shapes=[V((128, 768), BF16), V((512, 768), BF16), V((512, HD), F32), dma((4,)), dma((4,))],
+        scratch_shapes=[V((128, 768), BF16), V((512, 768), BF16), V((512, HD), F32), dma((6,)), dma((6,))],
         compiler_params=pltpu.CompilerParams(vmem_limit_bytes=62 * 2**20),
     )(*outs)
     return (keys[None], nw[None], nm[None])

time: 64.7 us -> 64.8 us (level)
  no operation moved by 1% of the time
where the time goes in v6:
time: 64.8 us; the launch traced here: 64.3 us
  Pallas kernels  63.7 us (98%)
    pallas_call x1, Pallas kernels, body(): pl.pallas_call(kernel, out_shape=shapes, in_specs=[hbm] * 7, out_specs=(h...  61.5 us
    pallas_call x1, Pallas kernels, body(): pl.pallas_call(finish, out_shape=shapes, in_specs=[hbm] * 3, out_specs=(h...  2.17 us

profile of v6, /device:TPU:1, one launch (start us, length us, event | category | flops | bytes accessed | tf_op | source)
XLA Modules:
  0.0 64.3 jit_solution(4761060590146144087)
XLA Ops:
  0.6 61.5 %shard_map.94 = (bf16[128,768]{1,0:T(8,128)(2,1)}, bf16[512,768]{1,0:T(8,128)(2,1)}, f32[512,128]{1,0:T(8,128)}) custom-call(bf16[128,8192]{1,0:T(8,128)(2,1)} %bitcast.10, f32[1,8192]{1,0:T(1,128)} %bitcast.14, bf16[4,128,768]{2,1,0:T(8,128)(2,1)} %bitcast.11, f32[512,128]{1,0:T(8,128)} %bitcast.12, bf16[128,768]{1,0:T(8,128)(2,1)} %bitcast.13, ...), custom_call_target="tpu_custom_call" | custom-call | tf_op jit(solution)/shard_map/pallas_call | solution.py:480
  62.1 2.2 %shard_map.95 = (bf16[128,768]{1,0:T(8,128)(2,1)}, bf16[512,768]{1,0:T(8,128)(2,1)}, f32[512,128]{1,0:T(8,128)}) custom-call(bf16[128,768]{1,0:T(8,128)(2,1)} %get-tuple-element.9.keys, bf16[512,768]{1,0:T(8,128)(2,1)} %get-tuple-element.10.nw, f32[512,128]{1,0:T(8,128)} %get-tuple-element.11.nm), custom_call_target="tpu_custom_call" | custom-call | tf_op jit(solution)/shard_map/pallas_call | solution.py:529
